TPU v7x, 32 devices: a whole 2x2x4 slice. The times are simulated.
32 devices in a mesh: dp: 2 (over y), expert: 16 (over z, x, core).
Axes of the slice: x: 2, y: 2, z: 4, core: 2. Of those that a mesh axis runs over, the one named last changes fastest.
Arguments:
- tokens: bfloat16 [1024, 2048], P(('dp', 'expert')), may hold values from -6 to 6
- routes: int32 [1024, 8], P(('dp', 'expert')), may hold values from 0 to 15, all different within a row; in each aligned block of 32 rows (0 to 31, 32 to 63, ...) at most 32 rows name the same one
- cotangent: bfloat16 [1024, 2048], P(('dp', 'expert')), may hold values from -6 to 6
- router_weight: bfloat16 [2048, 16], replicated, may hold values from -0.375 to 0.375
- gate_weight: bfloat16 [16, 2048, 768], P('expert'), may hold values from -0.125 to 0.125
- up_weight: bfloat16 [16, 2048, 768], P('expert'), may hold values from -0.125 to 0.125
- down_weight: bfloat16 [16, 768, 2048], P('expert'), may hold values from -0.21875 to 0.21875
Outputs:
- layer_out: bfloat16 [1024, 2048], P(('dp', 'expert'))
- token_grad: bfloat16 [1024, 2048], P(('dp', 'expert'))
- gate_grad: bfloat16 [16, 2048, 768], P('expert', 'dp')
- up_grad: bfloat16 [16, 2048, 768], P('expert', 'dp')
- down_grad: bfloat16 [16, 768, 2048], P('expert', None, 'dp')
- router_grad: float32 [2048, 16], replicated
Inputs may be any that keep to these rules, and one draw needn't show every extreme that they name: `routes`: each row names 8 different experts. Among the 32 rows of one device no expert is named by more than 32 rows, and in some device's rows an expert is named by exactly 32 rows.
All inputs are finite; a program needn't handle non-finite values.
Results may differ from a plain program's by a relative error of at most 0.0061.
Values may be sent and summed in bfloat16 or wider, within the bound.
A program may use at most 128 MiB of HBM per device.

v0:
```python
import jax
import jax.numpy as jnp
from jax import lax
from jax.sharding import PartitionSpec as P


def silu_parts(gate_act):
    sigmoid_value = jax.nn.sigmoid(gate_act)
    act_value = gate_act * sigmoid_value
    act_slope = sigmoid_value * (1.0 + gate_act * (1.0 - sigmoid_value))
    return (act_value, act_slope)


def expert_forward(arrived, gate_weight, up_weight, down_weight):
    gate_act = jnp.einsum(
        "sjcd,jdf->sjcf", arrived, gate_weight, preferred_element_type=jnp.float32
    )
    up_act = jnp.einsum("sjcd,jdf->sjcf", arrived, up_weight, preferred_element_type=jnp.float32)
    act_value, act_slope = silu_parts(gate_act)
    hidden = (act_value * up_act).astype(jnp.bfloat16)
    expert_out = jnp.einsum(
        "sjcf,jfd->sjcd", hidden, down_weight, preferred_element_type=jnp.float32
    ).astype(jnp.bfloat16)
    return (expert_out, (up_act, act_value, act_slope, hidden))


def expert_backward(arrived_grads, stored, gate_weight, up_weight, down_weight):
    up_act, act_value, act_slope, hidden = stored
    hidden_grad = jnp.einsum(
        "sjcd,jfd->sjcf", arrived_grads, down_weight, preferred_element_type=jnp.float32
    )
    gate_part = (hidden_grad * up_act * act_slope).astype(jnp.bfloat16)
    up_part = (hidden_grad * act_value).astype(jnp.bfloat16)
    input_grad = (
        jnp.einsum("sjcf,jdf->sjcd", gate_part, gate_weight, preferred_element_type=jnp.float32)
        + jnp.einsum("sjcf,jdf->sjcd", up_part, up_weight, preferred_element_type=jnp.float32)
    ).astype(jnp.bfloat16)
    return (input_grad, gate_part, up_part)


def local(tokens, routes, cotangent, router_weight, gate_weight, up_weight, down_weight):
    tok_rows, top_count = routes.shape
    model_width = tokens.shape[1]
    expert_count = router_weight.shape[1]
    local_count = gate_weight.shape[0]
    group_size = lax.axis_size("expert")
    capacity = min(tok_rows, 2 * tok_rows * top_count // expert_count)
    slot_total = expert_count * capacity
    buffer_shape = (group_size, local_count, capacity, model_width)
    logits = jnp.dot(tokens, router_weight, preferred_element_type=jnp.float32)
    exp_logits = jnp.exp(logits)
    probability = exp_logits / jnp.sum(exp_logits, axis=1, keepdims=True)
    chosen = (
        routes[:, :, None] == jnp.arange(expert_count, dtype=jnp.int32)[None, None, :]
    ).astype(jnp.int32)
    chosen_float = chosen.astype(jnp.float32)
    selected = jnp.sum(chosen_float * probability[:, None, :], axis=2)
    sel_total = jnp.sum(selected, axis=1, keepdims=True)
    combine = selected / sel_total
    per_token = jnp.sum(chosen, axis=1)
    earlier = jnp.cumsum(per_token, axis=0) - per_token
    slot_ids = jnp.sum(chosen * earlier[:, None, :], axis=2)
    flat_slot = routes * capacity + slot_ids
    match_map = (
        flat_slot[:, :, None] == jnp.arange(slot_total, dtype=jnp.int32)[None, None, :]
    ).astype(jnp.float32)
    presence = jnp.sum(match_map, axis=1)
    weight_map = jnp.sum(match_map * combine[:, :, None], axis=1)
    send_rows = (
        jnp.einsum(
            "tr,td->rd", presence.astype(jnp.bfloat16), tokens, preferred_element_type=jnp.float32
        )
        .astype(jnp.bfloat16)
        .reshape(buffer_shape)
    )
    send_grads = (
        jnp.einsum(
            "tr,td->rd", weight_map, cotangent.astype(jnp.float32), precision=lax.Precision.HIGHEST
        )
        .astype(jnp.bfloat16)
        .reshape(buffer_shape)
    )
    arrived = lax.all_to_all(send_rows, "expert", split_axis=0, concat_axis=0, tiled=True)
    expert_out, stored = expert_forward(arrived, gate_weight, up_weight, down_weight)
    returned = lax.all_to_all(expert_out, "expert", split_axis=0, concat_axis=0, tiled=True)
    arrived_grads = lax.all_to_all(send_grads, "expert", split_axis=0, concat_axis=0, tiled=True)
    input_grad, gate_part, up_part = expert_backward(
        arrived_grads, stored, gate_weight, up_weight, down_weight
    )
    returned_grads = lax.all_to_all(input_grad, "expert", split_axis=0, concat_axis=0, tiled=True)
    hidden = stored[3]
    gate_term = jnp.einsum("sjcd,sjcf->jdf", arrived, gate_part, preferred_element_type=jnp.float32)
    up_term = jnp.einsum("sjcd,sjcf->jdf", arrived, up_part, preferred_element_type=jnp.float32)
    down_term = jnp.einsum(
        "sjcf,sjcd->jfd", hidden, arrived_grads, preferred_element_type=jnp.float32
    )
    gate_sum, up_sum, down_sum = (
        lax.psum_scatter(gate_term, "dp", scatter_dimension=1, tiled=True),
        lax.psum_scatter(up_term, "dp", scatter_dimension=1, tiled=True),
        lax.psum_scatter(down_term, "dp", scatter_dimension=2, tiled=True),
    )
    gate_grad = gate_sum.astype(jnp.bfloat16)
    up_grad = up_sum.astype(jnp.bfloat16)
    down_grad = down_sum.astype(jnp.bfloat16)
    flat_index = flat_slot.reshape(-1)
    out_sel = jnp.take(returned.reshape(slot_total, model_width), flat_index, axis=0).reshape(
        tok_rows, top_count, model_width
    )
    grad_sel = jnp.take(
        returned_grads.reshape(slot_total, model_width), flat_index, axis=0
    ).reshape(tok_rows, top_count, model_width)
    layer_out = jnp.sum(combine[:, :, None] * out_sel.astype(jnp.float32), axis=1).astype(
        jnp.bfloat16
    )
    comb_grad = jnp.einsum("tkd,td->tk", out_sel, cotangent, preferred_element_type=jnp.float32)
    sel_grad = (comb_grad - jnp.sum(combine * comb_grad, axis=1, keepdims=True)) / sel_total
    prob_grad = jnp.sum(chosen_float * sel_grad[:, :, None], axis=1)
    logit_grad = probability * (prob_grad - jnp.sum(probability * prob_grad, axis=1, keepdims=True))
    router_term = jnp.einsum(
        "td,te->de", tokens.astype(jnp.float32), logit_grad, precision=lax.Precision.HIGHEST
    )
    router_grad = lax.psum(router_term, ("dp", "expert"))
    router_back = jnp.einsum(
        "te,de->td", logit_grad, router_weight.astype(jnp.float32), precision=lax.Precision.HIGHEST
    )
    token_grad = (jnp.sum(grad_sel.astype(jnp.float32), axis=1) + router_back).astype(jnp.bfloat16)
    return (layer_out, token_grad, gate_grad, up_grad, down_grad, router_grad)


def solution(mesh):
    return jax.shard_map(
        local,
        mesh=mesh,
        in_specs=(
            P(("dp", "expert"), None),
            P(("dp", "expert"), None),
            P(("dp", "expert"), None),
            P(),
            P("expert", None, None),
            P("expert", None, None),
            P("expert", None, None),
        ),
        out_specs=(
            P(("dp", "expert"), None),
            P(("dp", "expert"), None),
            P("expert", "dp", None),
            P("expert", "dp", None),
            P("expert", None, "dp"),
            P(),
        ),
        check_vma=False,
    )
```

profile of v0, /device:TPU:0, one launch (start us, length us, event | category | flops | bytes accessed | tf_op | source)
XLA Modules:
  0.0 455.1 jit_solution(14684139448227573478)
XLA Ops:
  8.9 1.1 fusion.55
  12.9 4.0 convolution_convert_fusion
  16.9 7.5 %all-to-all-start.2 = ((bf16[16,1,32,2048]{3,2,1,0:T(8,128)(2,1)}), bf16[16,1,32,2048]{3,2,1,0:T(8,128)(2,1)}, u32[]{:S(2)}, u32[]{:S(2)}) async-start(bf16[16,1,32,2048]{3,2,1,0:T(8,128)(2,1)} %bitcast.170), calls=%async_computation.2 | async-start | bytes 4194304 | tf_op jit(solution)/shard_map/all_to_all | solution.py:86
  24.5 2.1 convolution_convert_fusion.1
  26.6 39.1 %all-to-all-done.2 = bf16[16,1,32,2048]{3,2,1,0:T(8,128)(2,1)} async-done(((bf16[16,1,32,2048]{3,2,1,0:T(8,128)(2,1)}), bf16[16,1,32,2048]{3,2,1,0:T(8,128)(2,1)}, u32[]{:S(2)}, u32[]{:S(2)}) %all-to-all-start.2) | async-done | bytes 2097184 | tf_op jit(solution)/shard_map/all_to_all | solution.py:86
  65.7 11.3 %all-to-all-start = ((bf16[16,1,32,2048]{3,2,1,0:T(8,128)(2,1)}), bf16[16,1,32,2048]{3,2,1,0:T(8,128)(2,1)}, u32[]{:S(2)}, u32[]{:S(2)}) async-start(bf16[16,1,32,2048]{3,2,1,0:T(8,128)(2,1)} %bitcast.169), calls=%async_computation | async-start | bytes 4194304 | tf_op jit(solution)/shard_map/all_to_all | solution.py:83
  77.0 5.5 %fusion = f32[16,32,768]{2,1,0:T(8,128)} fusion(bf16[1,768,2048]{2,1,0:T(8,128)(2,1)} %param.15, bf16[16,1,32,2048]{3,2,1,0:T(8,128)(2,1)} %all-to-all-done.2), kind=kOutput, calls=%fused_computation.6 | convolution fusion | flops 1610612736 | bytes 6815744 | tf_op jit(solution)/shard_map/sjcd,jfd->sjcf/dot_general | solution.py:29
  82.5 35.6 %all-to-all-done = bf16[16,1,32,2048]{3,2,1,0:T(8,128)(2,1)} async-done(((bf16[16,1,32,2048]{3,2,1,0:T(8,128)(2,1)}), bf16[16,1,32,2048]{3,2,1,0:T(8,128)(2,1)}, u32[]{:S(2)}, u32[]{:S(2)}) %all-to-all-start) | async-done | bytes 2097184 | tf_op jit(solution)/shard_map/all_to_all | solution.py:83
  118.1 4.4 fusion.6
  122.5 5.1 %fusion.41 = (bf16[16,32,768]{2,1,0:T(8,128)(2,1)S(1)}, bf16[16,1,32,768]{3,2,0,1:T(8,128)(2,1)}, bf16[16,32,768]{2,1,0:T(8,128)(2,1)}) fusion(f32[16,32,768]{2,1,0:T(8,128)S(1)} %fusion.6, f32[16,32,768]{2,1,0:T(8,128)S(1)} %copy-done.6, bf16[1,2048,768]{2,1,0:T(8,128)(2,1)S(1)} %copy-done, bf16[16,1,32,2048]{3,2,1,0:T(8,128)(2,1)} %all-to-all-done), kind=kOutput, calls=%fused_computation.53 | convolution fusion | flops 1616510976 | bytes 10747904 | tf_op jit(solution)/shard_map/sjcd,jdf->sjcf/dot_general | solution.py:15
  128.5 6.1 %convolution_bitcast_fusion = f32[1,768,2048]{2,1,0:T(8,128)} fusion(bf16[16,32,768]{2,1,0:T(8,128)(2,1)S(1)} %get-tuple-element.13, bf16[16,1,32,2048]{3,2,1,0:T(8,128)(2,1)} %all-to-all-done.2), kind=kOutput, calls=%fused_computation.3 | convolution fusion | flops 1610612736 | bytes 9175040 | tf_op jit(solution)/shard_map/sjcf,sjcd->jfd/dot_general | solution.py:94
  134.7 6.3 %convolution_bitcast_fusion.2 = f32[1,2048,768]{2,1,0:T(8,128)} fusion(bf16[16,1,32,2048]{3,2,1,0:T(8,128)(2,1)} %all-to-all-done, bf16[16,1,32,768]{3,2,0,1:T(8,128)(2,1)} %get-tuple-element.14), kind=kOutput, calls=%fused_computation.5 | convolution fusion | flops 1610612736 | bytes 9175040 | tf_op jit(solution)/shard_map/sjcd,sjcf->jdf/dot_general | solution.py:92
  141.2 6.3 %convolution_bitcast_fusion.1 = f32[1,2048,768]{2,1,0:T(8,128)} fusion(bf16[16,32,768]{2,1,0:T(8,128)(2,1)} %get-tuple-element.15, bf16[16,1,32,2048]{3,2,1,0:T(8,128)(2,1)} %all-to-all-done), kind=kOutput, calls=%fused_computation.4 | convolution fusion | flops 1610612736 | bytes 9175040 | tf_op jit(solution)/shard_map/sjcd,sjcf->jdf/dot_general | solution.py:93
  147.5 5.6 %fusion.17 = bf16[16,1,32,2048]{3,2,1,0:T(8,128)(2,1)} fusion(bf16[16,32,768]{2,1,0:T(8,128)(2,1)} %copy-done.7, bf16[1,768,2048]{2,1,0:T(8,128)(2,1)} %param.15), kind=kOutput, calls=%fused_computation.21 | convolution fusion | flops 1611661312 | bytes 6029312 | tf_op jit(solution)/shard_map/sjcf,jfd->sjcd/dot_general | solution.py:21
  153.1 11.6 %all-to-all-start.1 = ((bf16[16,1,32,2048]{3,2,1,0:T(8,128)(2,1)}), bf16[16,1,32,2048]{3,2,1,0:T(8,128)(2,1)}, u32[]{:S(2)}, u32[]{:S(2)}) async-start(bf16[16,1,32,2048]{3,2,1,0:T(8,128)(2,1)} %fusion.17), calls=%async_computation.1 | async-start | bytes 4194304 | tf_op jit(solution)/shard_map/all_to_all | solution.py:85
  164.8 4.0 fusion.4
  168.8 3.1 fusion.20
  171.9 34.0 %all-to-all-done.1 = bf16[16,1,32,2048]{3,2,1,0:T(8,128)(2,1)} async-done(((bf16[16,1,32,2048]{3,2,1,0:T(8,128)(2,1)}), bf16[16,1,32,2048]{3,2,1,0:T(8,128)(2,1)}, u32[]{:S(2)}, u32[]{:S(2)}) %all-to-all-start.1) | async-done | bytes 2097184 | tf_op jit(solution)/shard_map/all_to_all | solution.py:85
  205.9 11.3 %all-to-all-start.3 = ((bf16[16,1,32,2048]{3,2,1,0:T(8,128)(2,1)}), bf16[16,1,32,2048]{3,2,1,0:T(8,128)(2,1)}, u32[]{:S(2)}, u32[]{:S(2)}) async-start(bf16[16,1,32,2048]{3,2,1,0:T(8,128)(2,1)} %fusion.20), calls=%async_computation.3 | async-start | bytes 4194304 | tf_op jit(solution)/shard_map/all_to_all | solution.py:90
  217.4 5.3 %gather_fusion = bf16[256,2048]{1,0:T(8,128)(2,1)} fusion(bf16[512,2048]{1,0:T(8,128)(2,1)} %bitcast.22, s32[1024]{0:T(1024)S(1)} %pad_clamp_fusion), kind=kCustom, calls=%fused_computation.clone | custom fusion | bytes 2098176 | tf_op jit(solution)/shard_map/jit(_take)/gather | solution.py:106
  222.7 2.1 fusion.39
  224.9 33.4 %all-to-all-done.3 = bf16[16,1,32,2048]{3,2,1,0:T(8,128)(2,1)} async-done(((bf16[16,1,32,2048]{3,2,1,0:T(8,128)(2,1)}), bf16[16,1,32,2048]{3,2,1,0:T(8,128)(2,1)}, u32[]{:S(2)}, u32[]{:S(2)}) %all-to-all-start.3) | async-done | bytes 2097184 | tf_op jit(solution)/shard_map/all_to_all | solution.py:90
  258.3 5.2 %gather_fusion.1 = bf16[256,2048]{1,0:T(8,128)(2,1)} fusion(bf16[512,2048]{1,0:T(8,128)(2,1)} %bitcast.40, s32[1024]{0:T(1024)S(1)} %pad_clamp_fusion), kind=kCustom, calls=%fused_computation.1.clone | custom fusion | bytes 2098176 | tf_op jit(solution)/shard_map/jit(_take)/gather | solution.py:109
  264.5 4.0 convert_reduce_fusion
  268.5 1.0 fusion.23
  269.5 3.3 convert_element_type.102
  272.7 25.2 %reduce-scatter.4.cloned.1.call-done = f32[1,1024,768]{2,1,0:T(8,128)} async-done(((f32[1,2048,768]{2,1,0:T(8,128)}), f32[1,1024,768]{2,1,0:T(8,128)}) %reduce-scatter.4.cloned.1.call-update) | async-done | bytes 3145744 | tf_op jit(solution)/shard_map/reduce_scatter | solution.py:98
  297.9 3.2 convert_element_type.100
  301.1 76.4 %reduce-scatter.6.cloned.1.call-done = f32[1,1024,768]{2,1,0:T(8,128)} async-done(((f32[1,2048,768]{2,1,0:T(8,128)}), f32[1,1024,768]{2,1,0:T(8,128)}) %reduce-scatter.6.cloned.1.call-update) | async-done | bytes 3145744 | tf_op jit(solution)/shard_map/reduce_scatter | solution.py:99
  377.6 3.2 convert_element_type.101
  380.8 65.6 %all-reduce.2.cloned.1.call-done = f32[2048,16]{0,1:T(8,128)} async-done(((f32[2048,16]{0,1:T(8,128)}), f32[2048,16]{0,1:T(8,128)}) %all-reduce.2.cloned.1.call-update) | async-done | bytes 131088 | tf_op jit(solution)/shard_map/psum | solution.py:122
  446.4 1.6 copy.44
  (48 shorter events, 6.2 us)
Async XLA Ops:
  8.0 114.5 %copy-start = (bf16[1,2048,768]{2,1,0:T(8,128)(2,1)S(1)}, bf16[1,2048,768]{2,1,0:T(8,128)(2,1)}, u32[]{:S(2)}) copy-start(bf16[1,2048,768]{2,1,0:T(8,128)(2,1)} %param.13) | copy-start | bytes 9437188
  16.9 7.6 %copy-start.1 = (bf16[32,2048]{1,0:T(8,128)(2,1)S(1)}, bf16[32,2048]{1,0:T(8,128)(2,1)}, u32[]{:S(2)}) copy-start(bf16[32,2048]{1,0:T(8,128)(2,1)} %param.9) | copy-start | bytes 393220
  16.9 48.7 %all-to-all-start.2 = ((bf16[16,1,32,2048]{3,2,1,0:T(8,128)(2,1)}), bf16[16,1,32,2048]{3,2,1,0:T(8,128)(2,1)}, u32[]{:S(2)}, u32[]{:S(2)}) async-start(bf16[16,1,32,2048]{3,2,1,0:T(8,128)(2,1)} %bitcast.170), calls=%async_computation.2 | async-start | bytes 4194304 | tf_op jit(solution)/shard_map/all_to_all | solution.py:86
  65.7 52.4 %all-to-all-start = ((bf16[16,1,32,2048]{3,2,1,0:T(8,128)(2,1)}), bf16[16,1,32,2048]{3,2,1,0:T(8,128)(2,1)}, u32[]{:S(2)}, u32[]{:S(2)}) async-start(bf16[16,1,32,2048]{3,2,1,0:T(8,128)(2,1)} %bitcast.169), calls=%async_computation | async-start | bytes 4194304 | tf_op jit(solution)/shard_map/all_to_all | solution.py:83
  76.9 192.5 %reduce-scatter.8.cloned.1.call-start = ((), (), s32[]{:S(2)}) async-start(), calls=%async_computation.9 | async-start | bytes 9437184 | tf_op jit(solution)/shard_map/reduce_scatter | solution.py:100
  118.1 4.4 copy-start.6
  127.6 0.9 copy-start.7
  134.6 163.3 %reduce-scatter.4.cloned.1.call-start = ((), (), s32[]{:S(2)}) async-start(), calls=%async_computation.7 | async-start | bytes 9437184 | tf_op jit(solution)/shard_map/reduce_scatter | solution.py:98
  141.0 236.6 %reduce-scatter.6.cloned.1.call-start = ((), (), s32[]{:S(2)}) async-start(), calls=%async_computation.8 | async-start | bytes 9437184 | tf_op jit(solution)/shard_map/reduce_scatter | solution.py:99
  153.1 52.8 %all-to-all-start.1 = ((bf16[16,1,32,2048]{3,2,1,0:T(8,128)(2,1)}), bf16[16,1,32,2048]{3,2,1,0:T(8,128)(2,1)}, u32[]{:S(2)}, u32[]{:S(2)}) async-start(bf16[16,1,32,2048]{3,2,1,0:T(8,128)(2,1)} %fusion.17), calls=%async_computation.1 | async-start | bytes 4194304 | tf_op jit(solution)/shard_map/all_to_all | solution.py:85
  164.7 4.0 copy-start.5
  205.9 52.4 %all-to-all-start.3 = ((bf16[16,1,32,2048]{3,2,1,0:T(8,128)(2,1)}), bf16[16,1,32,2048]{3,2,1,0:T(8,128)(2,1)}, u32[]{:S(2)}, u32[]{:S(2)}) async-start(bf16[16,1,32,2048]{3,2,1,0:T(8,128)(2,1)} %fusion.20), calls=%async_computation.3 | async-start | bytes 4194304 | tf_op jit(solution)/shard_map/all_to_all | solution.py:90
  217.2 229.2 %all-reduce.2.cloned.1.call-start = ((), (), s32[]{:S(2)}) async-start(), calls=%async_computation.10 | async-start | bytes 262144 | tf_op jit(solution)/shard_map/psum | solution.py:122
  217.4 5.4 %copy-start.3 = (bf16[32,2048]{1,0:T(8,128)(2,1)S(1)}, bf16[32,2048]{1,0:T(8,128)(2,1)}, u32[]{:S(2)}) copy-start(bf16[32,2048]{1,0:T(8,128)(2,1)} %param.11) | copy-start | bytes 393220
  258.3 5.2 %copy-start.4 = (s32[32,8]{0,1:T(8,128)S(1)}, s32[32,8]{0,1:T(8,128)}, u32[]{:S(2)}) copy-start(s32[32,8]{0,1:T(8,128)} %param.10) | copy-start | bytes 3076
  263.5 4.9 %copy-start.2 = (bf16[2048,16]{0,1:T(8,128)(2,1)S(1)}, bf16[2048,16]{0,1:T(8,128)(2,1)}, u32[]{:S(2)}) copy-start(bf16[2048,16]{0,1:T(8,128)(2,1)} %param.12) | copy-start | bytes 196612
Sparse Core Ops, SparseCore 0:
  134.7 83.5 reduce-scatter.7
  220.8 77.0 reduce-scatter.3
  300.2 77.2 reduce-scatter.5
Sparse Core Ops, SparseCore 1:
  268.6 177.8 all-reduce.1
where the time goes:
time: 456 us; the launch traced here: 455 us
  waiting for transfers between devices  309 us (68%)
  matrix products  57.6 us (13%)
  starting transfers between devices  42 us (9%)
  other arithmetic  17.2 us (4%)
  between operations  15.4 us (3%)
  local copies, waits for them, and re-layouts  13.5 us (3%)
    reduce_scatter x1, waiting for transfers between devices, local(): lax.psum_scatter(up_term, 'dp', scatter_dimension=1, tiled=True)  76.4 us
    psum x1, waiting for transfers between devices, local(): router_grad = lax.psum(router_term, ('dp', 'expert'))  65.6 us
    all_to_all x1, waiting for transfers between devices, local(): lax.all_to_all(send_grads, 'expert', split_axis=0, concat_axis=0, tiled=T...  39.1 us
    all_to_all x1, waiting for transfers between devices, local(): lax.all_to_all(send_rows, 'expert', split_axis=0, concat_axis=0, tiled=True)  35.6 us
    all_to_all x1, waiting for transfers between devices, local(): lax.all_to_all(expert_out, 'expert', split_axis=0, concat_axis=0, tiled=T...  34 us
    all_to_all x1, waiting for transfers between devices, local(): lax.all_to_all(input_grad, 'expert', split_axis=0, concat_axis=0, tiled=T...  33.4 us
    reduce_scatter x1, waiting for transfers between devices, local(): lax.psum_scatter(gate_term, 'dp', scatter_dimension=1, tiled=True)  25.2 us
    all_to_all x1, starting transfers between devices, local(): lax.all_to_all(expert_out, 'expert', split_axis=0, concat_axis=0, tiled=T...  11.6 us
  transfers between devices with their start and end apart: 8, of which 7 were waited for; matrix products, arithmetic and copies ran while one was open for 13% of the time, Pallas kernels for 0%

commit v1 on v0

--- a/solution.py
+++ b/solution.py
@@ -119,7 +119,8 @@
     router_term = jnp.einsum(
         "td,te->de", tokens.astype(jnp.float32), logit_grad, precision=lax.Precision.HIGHEST
     )
-    router_grad = lax.psum(router_term, ("dp", "expert"))
+    half = lax.psum(router_term, "expert")
+    router_grad = lax.psum(half, "dp")
     router_back = jnp.einsum(
         "te,de->td", logit_grad, router_weight.astype(jnp.float32), precision=lax.Precision.HIGHEST
     )

time: 456 us -> 475 us (1.042)
  blocking collectives: 0 us -> 59.9 us
  waiting for transfers between devices: 309 us -> 282 us
  starting transfers between devices: 42 us -> 30.5 us
    all_to_all x0 -> x1, blocking collectives: none -> 59.9 us  [local(): lax.all_to_all(input_grad, 'expert', split_axis=0, concat_axis=0, tiled=T...]
    reduce_scatter x1, waiting for transfers between devices: 25.2 us -> 66.6 us  [local(): lax.psum_scatter(gate_term, 'dp', scatter_dimension=1, tiled=True)]
    psum x1 -> x2, waiting for transfers between devices: 65.6 us -> 24.3 us  [the longest x1 20.4 us: local(): router_grad = lax.psum(half, 'dp')]
    all_to_all x1 -> x0, waiting for transfers between devices: 33.4 us -> none  [local(): lax.all_to_all(input_grad, 'expert', split_axis=0, concat_axis=0, tiled=T...]
    all_to_all x1 -> x0, starting transfers between devices: 11.3 us -> none  [local(): lax.all_to_all(input_grad, 'expert', split_axis=0, concat_axis=0, tiled=T...]
    all_to_all x1, waiting for transfers between devices: 34 us -> 40.8 us  [local(): lax.all_to_all(expert_out, 'expert', split_axis=0, concat_axis=0, tiled=T...]
  transfers between devices with their start and end apart: 8 -> 8, of which waited for: 7 -> 7; matrix products, arithmetic and copies ran while one was open for 13% -> 11% of each run, Pallas kernels for 0% -> 0%
where the time goes in v1:
time: 475 us; the launch traced here: 474 us
  waiting for transfers between devices  282 us (59%)
  blocking collectives  59.9 us (13%)
  matrix products  54.5 us (11%)
  starting transfers between devices  30.5 us (6%)
  other arithmetic  17.2 us (4%)
  between operations  15.9 us (3%)
  local copies, waits for them, and re-layouts  13.4 us (3%)
    reduce_scatter x1, waiting for transfers between devices, local(): lax.psum_scatter(up_term, 'dp', scatter_dimension=1, tiled=True)  76 us
    reduce_scatter x1, waiting for transfers between devices, local(): lax.psum_scatter(gate_term, 'dp', scatter_dimension=1, tiled=True)  66.6 us
    all_to_all x1, blocking collectives, local(): lax.all_to_all(input_grad, 'expert', split_axis=0, concat_axis=0, tiled=T...  59.9 us
    all_to_all x1, waiting for transfers between devices, local(): lax.all_to_all(expert_out, 'expert', split_axis=0, concat_axis=0, tiled=T...  40.8 us
    all_to_all x1, waiting for transfers between devices, local(): lax.all_to_all(send_grads, 'expert', split_axis=0, concat_axis=0, tiled=T...  39.1 us
    all_to_all x1, waiting for transfers between devices, local(): lax.all_to_all(send_rows, 'expert', split_axis=0, concat_axis=0, tiled=True)  35.7 us
    psum x1, waiting for transfers between devices, local(): router_grad = lax.psum(half, 'dp')  20.4 us
    all_to_all x1, starting transfers between devices, local(): lax.all_to_all(expert_out, 'expert', split_axis=0, concat_axis=0, tiled=T...  11.3 us
  transfers between devices with their start and end apart: 8, of which 7 were waited for; matrix products, arithmetic and copies ran while one was open for 11% of the time, Pallas kernels for 0%

profile of v1, /device:TPU:0, one launch (start us, length us, event | category | flops | bytes accessed | tf_op | source)
XLA Modules:
  0.0 473.9 jit_solution(11631644277656374392)
XLA Ops:
  8.9 1.1 fusion.55
  12.9 4.0 convolution_convert_fusion
  16.9 7.5 %all-to-all-start.2 = ((bf16[16,1,32,2048]{3,2,1,0:T(8,128)(2,1)}), bf16[16,1,32,2048]{3,2,1,0:T(8,128)(2,1)}, u32[]{:S(2)}, u32[]{:S(2)}) async-start(bf16[16,1,32,2048]{3,2,1,0:T(8,128)(2,1)} %bitcast.171), calls=%async_computation.2 | async-start | bytes 4194304 | tf_op jit(solution)/shard_map/all_to_all | solution.py:86
  24.5 2.1 convolution_convert_fusion.1
  26.6 39.1 %all-to-all-done.2 = bf16[16,1,32,2048]{3,2,1,0:T(8,128)(2,1)} async-done(((bf16[16,1,32,2048]{3,2,1,0:T(8,128)(2,1)}), bf16[16,1,32,2048]{3,2,1,0:T(8,128)(2,1)}, u32[]{:S(2)}, u32[]{:S(2)}) %all-to-all-start.2) | async-done | bytes 2097184 | tf_op jit(solution)/shard_map/all_to_all | solution.py:86
  65.7 11.3 %all-to-all-start = ((bf16[16,1,32,2048]{3,2,1,0:T(8,128)(2,1)}), bf16[16,1,32,2048]{3,2,1,0:T(8,128)(2,1)}, u32[]{:S(2)}, u32[]{:S(2)}) async-start(bf16[16,1,32,2048]{3,2,1,0:T(8,128)(2,1)} %bitcast.170), calls=%async_computation | async-start | bytes 4194304 | tf_op jit(solution)/shard_map/all_to_all | solution.py:83
  76.9 5.5 %fusion = f32[16,32,768]{2,1,0:T(8,128)} fusion(bf16[1,768,2048]{2,1,0:T(8,128)(2,1)} %param.15, bf16[16,1,32,2048]{3,2,1,0:T(8,128)(2,1)} %all-to-all-done.2), kind=kOutput, calls=%fused_computation.6 | convolution fusion | flops 1610612736 | bytes 6815744 | tf_op jit(solution)/shard_map/sjcd,jfd->sjcf/dot_general | solution.py:29
  82.4 35.7 %all-to-all-done = bf16[16,1,32,2048]{3,2,1,0:T(8,128)(2,1)} async-done(((bf16[16,1,32,2048]{3,2,1,0:T(8,128)(2,1)}), bf16[16,1,32,2048]{3,2,1,0:T(8,128)(2,1)}, u32[]{:S(2)}, u32[]{:S(2)}) %all-to-all-start) | async-done | bytes 2097184 | tf_op jit(solution)/shard_map/all_to_all | solution.py:83
  118.1 4.4 fusion.6
  122.6 5.2 %fusion.41 = (bf16[16,32,768]{2,1,0:T(8,128)(2,1)S(1)}, bf16[16,1,32,768]{3,2,0,1:T(8,128)(2,1)}, bf16[16,32,768]{2,1,0:T(8,128)(2,1)}) fusion(f32[16,32,768]{2,1,0:T(8,128)S(1)} %fusion.6, f32[16,32,768]{2,1,0:T(8,128)S(1)} %copy-done.7, bf16[1,2048,768]{2,1,0:T(8,128)(2,1)S(1)} %copy-done, bf16[16,1,32,2048]{3,2,1,0:T(8,128)(2,1)} %all-to-all-done), kind=kOutput, calls=%fused_computation.53 | convolution fusion | flops 1616510976 | bytes 10747904 | tf_op jit(solution)/shard_map/sjcd,jdf->sjcf/dot_general | solution.py:15
  128.7 3.1 fusion.17
  131.8 11.3 %all-to-all-start.1 = ((bf16[16,1,32,2048]{3,2,1,0:T(8,128)(2,1)}), bf16[16,1,32,2048]{3,2,1,0:T(8,128)(2,1)}, u32[]{:S(2)}, u32[]{:S(2)}) async-start(bf16[16,1,32,2048]{3,2,1,0:T(8,128)(2,1)} %fusion.17), calls=%async_computation.1 | async-start | bytes 4194304 | tf_op jit(solution)/shard_map/all_to_all | solution.py:85
  143.4 40.8 %all-to-all-done.1 = bf16[16,1,32,2048]{3,2,1,0:T(8,128)(2,1)} async-done(((bf16[16,1,32,2048]{3,2,1,0:T(8,128)(2,1)}), bf16[16,1,32,2048]{3,2,1,0:T(8,128)(2,1)}, u32[]{:S(2)}, u32[]{:S(2)}) %all-to-all-start.1) | async-done | bytes 2097184 | tf_op jit(solution)/shard_map/all_to_all | solution.py:85
  184.3 5.2 %gather_fusion = bf16[256,2048]{1,0:T(8,128)(2,1)} fusion(bf16[512,2048]{1,0:T(8,128)(2,1)} %bitcast.22, s32[1024]{0:T(1024)S(1)} %pad_clamp_fusion), kind=kCustom, calls=%fused_computation.clone | custom fusion | bytes 2098176 | tf_op jit(solution)/shard_map/jit(_take)/gather | solution.py:106
  189.5 2.2 fusion.39
  192.8 6.3 %convolution_bitcast_fusion = f32[1,768,2048]{2,1,0:T(8,128)} fusion(bf16[16,32,768]{2,1,0:T(8,128)(2,1)} %copy-done.8, bf16[16,1,32,2048]{3,2,1,0:T(8,128)(2,1)} %all-to-all-done.2), kind=kOutput, calls=%fused_computation.3 | convolution fusion | flops 1610612736 | bytes 9175040 | tf_op jit(solution)/shard_map/sjcf,sjcd->jfd/dot_general | solution.py:94
  199.2 6.3 %convolution_bitcast_fusion.2 = f32[1,2048,768]{2,1,0:T(8,128)} fusion(bf16[16,1,32,2048]{3,2,1,0:T(8,128)(2,1)} %all-to-all-done, bf16[16,1,32,768]{3,2,0,1:T(8,128)(2,1)} %get-tuple-element.14), kind=kOutput, calls=%fused_computation.5 | convolution fusion | flops 1610612736 | bytes 9175040 | tf_op jit(solution)/shard_map/sjcd,sjcf->jdf/dot_general | solution.py:92
  205.5 6.2 %convolution_bitcast_fusion.1 = f32[1,2048,768]{2,1,0:T(8,128)} fusion(bf16[16,32,768]{2,1,0:T(8,128)(2,1)} %get-tuple-element.15, bf16[16,1,32,2048]{3,2,1,0:T(8,128)(2,1)} %all-to-all-done), kind=kOutput, calls=%fused_computation.4 | convolution fusion | flops 1610612736 | bytes 9175040 | tf_op jit(solution)/shard_map/sjcd,sjcf->jdf/dot_general | solution.py:93
  211.8 4.4 fusion.4
  216.3 1.8 fusion.20
  218.1 59.9 %all_to_all.20 = bf16[16,1,32,2048]{3,2,1,0:T(8,128)(2,1)} all-to-all(bf16[16,1,32,2048]{3,2,1,0:T(8,128)(2,1)S(1)} %fusion.20), channel_id=1, replica_groups=mesh['dp'=2,'expert'=16] {'expert'}, dimensions={0} | all-to-all | bytes 4194304 | tf_op jit(solution)/shard_map/all_to_all | solution.py:90
  278.0 5.2 %gather_fusion.1 = bf16[256,2048]{1,0:T(8,128)(2,1)} fusion(bf16[512,2048]{1,0:T(8,128)(2,1)} %bitcast.169, s32[1024]{0:T(1024)S(1)} %pad_clamp_fusion), kind=kCustom, calls=%fused_computation.1.clone | custom fusion | bytes 2098176 | tf_op jit(solution)/shard_map/jit(_take)/gather | solution.py:109
  283.2 3.9 convert_reduce_fusion
  287.1 3.9 all-reduce.3.cloned.1.call-done
  291.1 1.0 fusion.23
  292.1 3.4 convert_element_type.102
  295.4 66.6 %reduce-scatter.4.cloned.1.call-done = f32[1,1024,768]{2,1,0:T(8,128)} async-done(((f32[1,2048,768]{2,1,0:T(8,128)}), f32[1,1024,768]{2,1,0:T(8,128)}) %reduce-scatter.4.cloned.1.call-update) | async-done | bytes 3145744 | tf_op jit(solution)/shard_map/reduce_scatter | solution.py:98
  362.0 3.2 convert_element_type.100
  365.2 76.0 %reduce-scatter.6.cloned.1.call-done = f32[1,1024,768]{2,1,0:T(8,128)} async-done(((f32[1,2048,768]{2,1,0:T(8,128)}), f32[1,1024,768]{2,1,0:T(8,128)}) %reduce-scatter.6.cloned.1.call-update) | async-done | bytes 3145744 | tf_op jit(solution)/shard_map/reduce_scatter | solution.py:99
  441.2 3.2 convert_element_type.101
  444.4 20.4 %all-reduce.5.cloned.1.call-done = f32[2048,16]{0,1:T(8,128)} async-done(((f32[2048,16]{0,1:T(8,128)}), f32[2048,16]{0,1:T(8,128)}) %all-reduce.5.cloned.1.call-update) | async-done | bytes 131088 | tf_op jit(solution)/shard_map/psum | solution.py:123
  464.7 1.6 copy.45
  (52 shorter events, 6.3 us)
Async XLA Ops:
  8.0 114.5 %copy-start = (bf16[1,2048,768]{2,1,0:T(8,128)(2,1)S(1)}, bf16[1,2048,768]{2,1,0:T(8,128)(2,1)}, u32[]{:S(2)}) copy-start(bf16[1,2048,768]{2,1,0:T(8,128)(2,1)} %param.13) | copy-start | bytes 9437188
  16.9 7.6 %copy-start.1 = (bf16[32,2048]{1,0:T(8,128)(2,1)S(1)}, bf16[32,2048]{1,0:T(8,128)(2,1)}, u32[]{:S(2)}) copy-start(bf16[32,2048]{1,0:T(8,128)(2,1)} %param.9) | copy-start | bytes 393220
  16.9 48.7 %all-to-all-start.2 = ((bf16[16,1,32,2048]{3,2,1,0:T(8,128)(2,1)}), bf16[16,1,32,2048]{3,2,1,0:T(8,128)(2,1)}, u32[]{:S(2)}, u32[]{:S(2)}) async-start(bf16[16,1,32,2048]{3,2,1,0:T(8,128)(2,1)} %bitcast.171), calls=%async_computation.2 | async-start | bytes 4194304 | tf_op jit(solution)/shard_map/all_to_all | solution.py:86
  65.7 52.4 %all-to-all-start = ((bf16[16,1,32,2048]{3,2,1,0:T(8,128)(2,1)}), bf16[16,1,32,2048]{3,2,1,0:T(8,128)(2,1)}, u32[]{:S(2)}, u32[]{:S(2)}) async-start(bf16[16,1,32,2048]{3,2,1,0:T(8,128)(2,1)} %bitcast.170), calls=%async_computation | async-start | bytes 4194304 | tf_op jit(solution)/shard_map/all_to_all | solution.py:83
  118.1 4.4 copy-start.7
  122.5 6.2 %copy-start.5 = (bf16[1,768,2048]{2,1,0:T(8,128)(2,1)S(1)}, bf16[1,768,2048]{2,1,0:T(8,128)(2,1)}, u32[]{:S(2)}) copy-start(bf16[1,768,2048]{2,1,0:T(8,128)(2,1)} %param.15) | copy-start | bytes 9437188
  127.8 0.9 copy-start.8
  131.8 52.4 %all-to-all-start.1 = ((bf16[16,1,32,2048]{3,2,1,0:T(8,128)(2,1)}), bf16[16,1,32,2048]{3,2,1,0:T(8,128)(2,1)}, u32[]{:S(2)}, u32[]{:S(2)}) async-start(bf16[16,1,32,2048]{3,2,1,0:T(8,128)(2,1)} %fusion.17), calls=%async_computation.1 | async-start | bytes 4194304 | tf_op jit(solution)/shard_map/all_to_all | solution.py:85
  143.1 148.0 %all-reduce.3.cloned.1.call-start = ((), (), s32[]{:S(2)}) async-start(), calls=%async_computation.10 | async-start | bytes 262144 | tf_op jit(solution)/shard_map/psum | solution.py:122
  184.3 5.2 %copy-start.3 = (bf16[32,2048]{1,0:T(8,128)(2,1)S(1)}, bf16[32,2048]{1,0:T(8,128)(2,1)}, u32[]{:S(2)}) copy-start(bf16[32,2048]{1,0:T(8,128)(2,1)} %param.11) | copy-start | bytes 393220
  189.5 2.3 copy-start.4
  192.7 99.4 %reduce-scatter.8.cloned.1.call-start = ((), (), s32[]{:S(2)}) async-start(), calls=%async_computation.9 | async-start | bytes 9437184 | tf_op jit(solution)/shard_map/reduce_scatter | solution.py:100
  199.1 162.9 %reduce-scatter.4.cloned.1.call-start = ((), (), s32[]{:S(2)}) async-start(), calls=%async_computation.7 | async-start | bytes 9437184 | tf_op jit(solution)/shard_map/reduce_scatter | solution.py:98
  205.4 235.7 %reduce-scatter.6.cloned.1.call-start = ((), (), s32[]{:S(2)}) async-start(), calls=%async_computation.8 | async-start | bytes 9437184 | tf_op jit(solution)/shard_map/reduce_scatter | solution.py:99
  211.7 253.0 %all-reduce.5.cloned.1.call-start = ((), (), s32[]{:S(2)}) async-start(), calls=%async_computation.11 | async-start | bytes 262144 | tf_op jit(solution)/shard_map/psum | solution.py:123
  211.8 4.5 copy-start.6
  283.2 7.9 %copy-start.2 = (bf16[2048,16]{0,1:T(8,128)(2,1)S(1)}, bf16[2048,16]{0,1:T(8,128)(2,1)}, u32[]{:S(2)}) copy-start(bf16[2048,16]{0,1:T(8,128)(2,1)} %param.12) | copy-start | bytes 196612
Sparse Core Ops, SparseCore 0:
  192.8 98.1 all-reduce.2
Sparse Core Ops, SparseCore 1:
  199.2 83.5 reduce-scatter.7
  285.0 77.0 reduce-scatter.3
  364.2 76.9 reduce-scatter.5
  443.5 21.1 all-reduce.4
